TPU v7x, 32 devices: a whole 2x2x4 slice. The times are simulated.
32 devices in a mesh: grp: 4 (over y, x), dev: 8 (over z, core).
Axes of the slice: x: 2, y: 2, z: 4, core: 2. Of those that a mesh axis runs over, the one named last changes fastest.
Arguments:
- positions: float32 [3, 8192], P(None, ('grp', 'dev')), may hold values from -1 to 1
- velocities: float32 [3, 8192], P(None, ('grp', 'dev')), may hold values from -4 to 4
- accel_old: float32 [3, 8192], P(None, ('grp', 'dev')), may hold values from -6 to 6
- jerk_old: float32 [3, 8192], P(None, ('grp', 'dev')), may hold values from -6 to 6
- masses: float32 [8192], P(('grp', 'dev')), may hold values from 2.4414063e-05 to 0.00061035156
- levels: int32 [8192], P(('grp', 'dev')), may hold values from 0 to 3
- live_count: int32 [32], P(('grp', 'dev')), may hold values from 128 to 256, as said below
- active_slot: int32 [4096], P(('grp', 'dev')), may hold values from 0 to 255, as said below
Outputs:
- pos_vel: float32 [6, 4096], P(None, ('grp', 'dev'))
- acc_jerk: float32 [6, 4096], P(None, ('grp', 'dev'))
- potential: float32 [4096], P(('grp', 'dev'))
Inputs may be any that keep to these rules, and one draw needn't show every extreme that they name: `live_count`: every entry is at least 128; some device is full with 256 and some has exactly 128; the counts are uneven across devices. `active_slot`: within each device's aligned block of 128 entries the slots are distinct and below that device's live_count.
All inputs are finite; a program needn't handle non-finite values.
Results may differ from a plain program's by a relative error of at most 0.00029.
Values sent between devices are 32-bit elements; how exact they have to be, the bound alone decides.
A program may use at most 64 MiB of HBM per device.

v0:
```python
import functools
import math

import jax
import jax.numpy as jnp
from jax import lax
from jax.experimental import pallas as pl
from jax.experimental.pallas import tpu as pltpu
from jax.sharding import PartitionSpec as P

MESH = pl.DeviceIdType.MESH
LANES = 128
TAU_BASE = 0.5
SOFTEN_SQ = 0.0001


def add_pairs(state, sums, source):
    x, y, z, vx, vy, vz = state
    ax, ay, az, jx, jy, jz, pot = sums
    sx, sy, sz, svx, svy, svz, mass = source
    dx, dy, dz = sx - x, sy - y, sz - z
    ex, ey, ez = svx - vx, svy - vy, svz - vz
    inv = lax.rsqrt(dx * dx + dy * dy + dz * dz + SOFTEN_SQ)
    inv_sq = inv * inv
    w = mass * inv
    u = w * inv_sq
    radial = (3.0 * inv_sq) * (dx * ex + dy * ey + dz * ez)
    px, py, pz = u * dx, u * dy, u * dz
    return (
        ax + px, ay + py, az + pz,
        jx + (u * ex - radial * px), jy + (u * ey - radial * py), jz + (u * ez - radial * pz),
        pot + w,
    )


def sweep(act, total, rows, chunks):
    def group(g, carry):
        at = pl.ds(pl.multiple_of(g * rows, rows), rows)
        state = [act[c, at, :] for c in range(6)]
        sums = tuple(total[c, at, :] for c in range(7))
        for chunk in chunks:
            sums = add_pairs(state, sums, [chunk(c) for c in range(7)])
        for c in range(7):
            total[c, at, :] = sums[c]
        return carry

    lax.fori_loop(0, act.shape[1] // rows, group, 0)


def spread(own, act):
    for c in range(6):
        act[c] = jnp.broadcast_to(own[c : c + 1, :], (LANES, own.shape[1])).T


def share(
    n_grp, n_line, n_core, rows, batch,
    pos_hbm, vel_hbm, acc_hbm, jerk_hbm, mass_hbm, level_hbm, live_hbm, slot_hbm,
    beyond_hbm, total_hbm, own_hbm,
    pos_ref, vel_ref, acc_ref, jerk_ref, mass_ref, level_ref, live_ref, slot_ref,
    src, act, total, own, rest,
    load_sem, line_send, line_recv, grp_send, grp_recv, core_send, core_recv, beyond_sem, out_sem,
):
    n_src = pos_ref.shape[1]
    n_act = slot_ref.shape[1]
    n_chunk = n_src // LANES
    grp = lax.axis_index("grp")
    dev = lax.axis_index("dev")
    line, core = dev // n_core, lax.rem(dev, n_core)
    twin = n_core - 1 - core

    loads = [
        pltpu.make_async_copy(there, here, load_sem.at[i])
        for i, (there, here) in enumerate((
            (pos_hbm, pos_ref), (vel_hbm, vel_ref), (acc_hbm, acc_ref), (jerk_hbm, jerk_ref),
            (mass_hbm, mass_ref), (level_hbm, level_ref), (live_hbm, live_ref), (slot_hbm, slot_ref),
        ))
    ]
    for load in loads:
        load.start()

    def on_line(k):
        return lax.rem(line + k, n_line)

    def on_grp(k):
        return lax.rem(grp + k, n_grp)

    def each(count, body):
        def one(k, carry):
            body(k)
            return carry

        lax.fori_loop(1, count, one, 0)

    barrier = pltpu.get_barrier_semaphore()

    def greet(place):
        pl.semaphore_signal(barrier, inc=1, device_id=place, device_id_type=MESH)

    each(n_line, lambda k: greet((grp, on_line(k) * n_core + core)))
    each(n_grp, lambda k: greet((on_grp(k), dev)))
    if n_core > 1:
        greet((grp, line * n_core + twin))
    total[...] = jnp.zeros_like(total)
    for load in loads:
        load.wait()

    mine = src.at[core, grp, line]
    level = level_ref[...]
    step = jnp.full(level.shape, TAU_BASE, jnp.float32)
    step = jnp.where((level & 1) != 0, step * 0.5, step)
    step = jnp.where((level & 2) != 0, step * 0.25, step)
    step = jnp.where((level & 4) != 0, step * 0.0625, step)
    vel, acc, jerk = vel_ref[...], acc_ref[...], jerk_ref[...]
    pos_pred = pos_ref[...] + step * (vel + step * (acc * 0.5 + step * jerk * (1.0 / 6.0)))
    vel_pred = vel + step * (acc + step * jerk * 0.5)
    lane = lax.broadcasted_iota(jnp.int32, (1, n_src), 1)
    live = jnp.full((1, n_src), live_ref[0], jnp.int32)
    live_mass = jnp.where(lane < live, mass_ref[...], 0.0)
    count = live.astype(jnp.float32)
    for chunk in range(n_chunk):
        cut = slice(chunk * LANES, (chunk + 1) * LANES)
        mine[chunk, 0:3, :] = pos_pred[:, cut]
        mine[chunk, 3:6, :] = vel_pred[:, cut]
        mine[chunk, 6:7, :] = live_mass[:, cut]
        mine[chunk, 7:8, :] = count[:, cut]
    rest[0:3, :] = acc
    rest[3:6, :] = jerk
    rest[6:7, :] = step
    rest[7:8, :] = jnp.zeros_like(step)

    pl.semaphore_wait(barrier, (n_line - 1) + (n_grp - 1) + (n_core - 1))

    def line_copy(origin, other):
        block = src.at[core, grp, origin]
        return pltpu.make_async_remote_copy(
            src_ref=block, dst_ref=block,
            send_sem=line_send.at[other], recv_sem=line_recv.at[origin],
            device_id=(grp, other * n_core + core), device_id_type=MESH,
        )

    def grp_copy(at, origin, other):
        block = src.at[core, origin, at]
        return pltpu.make_async_remote_copy(
            src_ref=block, dst_ref=block,
            send_sem=grp_send.at[at, other], recv_sem=grp_recv.at[at, origin],
            device_id=(other, dev), device_id_type=MESH,
        )

    def to_groups(at):
        each(n_grp, lambda k: grp_copy(at, grp, on_grp(k)).start())

    def core_copy(owner, origin):
        block = src.at[owner, origin]
        return pltpu.make_async_remote_copy(
            src_ref=block, dst_ref=block,
            send_sem=core_send.at[origin], recv_sem=core_recv.at[origin],
            device_id=(grp, line * n_core + twin), device_id_type=MESH,
        )

    def keep(owner, origin):
        return pltpu.make_async_copy(
            src.at[owner, origin, :, 1:], beyond_hbm.at[owner, origin], beyond_sem.at[owner, origin]
        )

    def add(owner, origin):
        def turn(t, carry):
            sweep(act, total, rows, [
                lambda c, at=t * batch + b: src[owner, origin, at, 0, c : c + 1, :]
                for b in range(batch)
            ])
            return carry

        lax.fori_loop(0, n_line // batch, turn, 0)

    each(n_line, lambda k: line_copy(line, on_line(k)).start())
    to_groups(line)

    slot = jnp.broadcast_to(slot_ref[...], (8, n_act))
    low, part = slot & (LANES - 1), slot // LANES

    def pick(chunk_of):
        out = jnp.zeros((8, n_act), jnp.float32)
        for chunk in range(n_chunk):
            found = jnp.take_along_axis(chunk_of(chunk), low, axis=1)
            out = jnp.where(part == chunk, found, out)
        return out

    state = pick(lambda chunk: mine[chunk])
    own[0:8, :] = state
    own[8:16, :] = pick(lambda chunk: rest[:, chunk * LANES : (chunk + 1) * LANES])
    own_copy = pltpu.make_async_copy(own, own_hbm, out_sem.at[0])
    own_copy.start()
    spread(own, act)

    def pass_on(k):
        line_copy(on_line(k), on_line(k)).wait_recv()
        to_groups(on_line(k))

    each(n_line, pass_on)
    if n_core > 1:
        core_copy(core, grp).start()
    keep(core, grp).start()
    add(core, grp)
    if n_core > 1:
        core_copy(twin, grp).wait_recv()
        keep(twin, grp).start()
        add(twin, grp)

    def forward(k):
        origin = on_grp(k)
        grp_copy(line, origin, origin).wait_recv()
        each(n_line, lambda at: grp_copy(on_line(at), origin, origin).wait_recv())
        if n_core > 1:
            core_copy(core, origin).start()
        keep(core, origin).start()

    each(n_grp, forward)
    each(n_grp, lambda k: add(core, on_grp(k)))

    if n_core > 1:
        def last(k):
            origin = on_grp(k)
            core_copy(twin, origin).wait_recv()
            keep(twin, origin).start()
            add(twin, origin)

        each(n_grp, last)

    total_copy = pltpu.make_async_copy(total, total_hbm, out_sem.at[1])
    total_copy.start()
    each(n_line, lambda k: line_copy(line, on_line(k)).wait_send())

    def sent(at, carry):
        each(n_grp, lambda k: grp_copy(at, grp, on_grp(k)).wait_send())
        return carry

    lax.fori_loop(0, n_line, sent, 0)

    def settle(origin, carry):
        if n_core > 1:
            core_copy(core, origin).wait_send()
        for owner in range(n_core):
            keep(owner, origin).wait()
        return carry

    lax.fori_loop(0, n_grp, settle, 0)
    own_copy.wait()
    total_copy.wait()


def finish(
    rows, batch,
    beyond_hbm, total_hbm, own_hbm,
    pos_vel_hbm, acc_jerk_hbm, pot_hbm,
    beyond, total, own, act, packed, more, pos_vel_ref, acc_jerk_ref, pot_ref, load_sem, store_sem,
):
    n, n_beyond = beyond.shape[0], beyond.shape[1]
    loads = [
        pltpu.make_async_copy(there, here, load_sem.at[i])
        for i, (there, here) in enumerate(((own_hbm, own), (beyond_hbm, beyond), (total_hbm, total)))
    ]
    for load in loads:
        load.start()
    lane = lax.broadcasted_iota(jnp.int32, (8, LANES), 1)
    row = lax.broadcasted_iota(jnp.int32, (8, LANES), 0)
    more[...] = jnp.zeros_like(more)
    loads[0].wait()
    spread(own, act)
    loads[1].wait()

    unroll = math.gcd(8, n)

    def pack(turn, carry):
        filled, now = carry
        counts = [beyond[turn * unroll + b, 0, 7, 0].astype(jnp.int32) for b in range(unroll)]
        for b in range(unroll):
            for chunk in range(n_beyond):
                many = jnp.minimum(jnp.maximum(counts[b] - (chunk + 1) * LANES, 0), LANES)
                start = lax.rem(filled, LANES)
                moved = pltpu.roll(beyond[turn * unroll + b, chunk], start, 1)
                now = jnp.where(lane >= start, moved, now)
                packed[filled // LANES] = now
                now = jnp.where(start + many >= LANES, moved, now)
                filled = filled + many
        return filled, now

    filled, now = lax.fori_loop(
        0, n // unroll, pack, (jnp.int32(0), jnp.zeros((8, LANES), jnp.float32))
    )
    last = filled // LANES
    packed[last] = jnp.where((row == 6) & (lane >= lax.rem(filled, LANES)), 0.0, now)
    for b in range(1, batch):
        packed[last + b] = jnp.zeros((8, LANES), jnp.float32)

    def turns(turn, carry):
        sweep(act, more, rows, [
            lambda c, at=turn * batch + b: packed[at, c : c + 1, :] for b in range(batch)
        ])
        return carry

    lax.fori_loop(0, (filled + batch * LANES - 1) // (batch * LANES), turns, 0)

    loads[2].wait()
    for c in range(6):
        acc_jerk_ref[c : c + 1, :] = jnp.sum((total[c] + more[c]).T, axis=0, keepdims=True)
    pot_ref[...] = -jnp.sum((total[6] + more[6]).T, axis=0, keepdims=True)
    stores = [
        pltpu.make_async_copy(here, there, store_sem.at[i])
        for i, (here, there) in enumerate((
            (acc_jerk_ref, acc_jerk_hbm), (pot_ref, pot_hbm), (pos_vel_ref, pos_vel_hbm),
        ))
    ]
    stores[0].start()
    stores[1].start()

    acc_end, jerk_end = acc_jerk_ref[0:3, :], acc_jerk_ref[3:6, :]
    pos_now, vel_now = own[0:3, :], own[3:6, :]
    acc_start, jerk_start, h = own[8:11, :], own[11:14, :], own[14:15, :]
    differ = acc_start - acc_end
    fourth = -6.0 * differ - h * (4.0 * jerk_start + 2.0 * jerk_end)
    fifth = 12.0 * differ + 6.0 * h * (jerk_start + jerk_end)
    pos_vel_ref[0:3, :] = pos_now + h * h * (1.0 / 24.0) * fourth + h * h * (1.0 / 120.0) * fifth
    pos_vel_ref[3:6, :] = vel_now + h * (1.0 / 6.0) * fourth + h * (1.0 / 24.0) * fifth
    stores[2].start()
    for store in stores:
        store.wait()


def solution(mesh):
    n_grp, n_dev = mesh.shape["grp"], mesh.shape["dev"]
    n = n_grp * n_dev

    def shards(positions, velocities, accel_old, jerk_old, masses, levels, live_count, active_slot):
        n_src, n_act = positions.shape[1], active_slot.shape[0]
        n_chunk = n_src // LANES
        hbm = pl.BlockSpec(memory_space=pltpu.HBM)
        args = (
            positions, velocities, accel_old, jerk_old,
            masses[None], levels[None], live_count, active_slot[None],
        )
        f32 = jnp.float32
        n_core = math.gcd(2, n_dev)
        n_line = n_dev // n_core
        dma = pltpu.SemaphoreType.DMA
        beyond, total, own = pl.pallas_call(
            functools.partial(
                share, n_grp, n_line, n_core, math.gcd(16, n_act), math.gcd(4, n_line)
            ),
            out_shape=(
                jax.ShapeDtypeStruct((n_core, n_grp, n_line, n_chunk - 1, 8, LANES), f32),
                jax.ShapeDtypeStruct((7, n_act, LANES), f32),
                jax.ShapeDtypeStruct((16, n_act), f32),
            ),
            in_specs=[hbm] * 8,
            out_specs=(hbm,) * 3,
            scratch_shapes=[
                (pltpu.SMEM if a is live_count else pltpu.VMEM)(a.shape, a.dtype) for a in args
            ] + [
                pltpu.VMEM((n_core, n_grp, n_line, n_chunk, 8, LANES), f32),
                pltpu.VMEM((6, n_act, LANES), f32),
                pltpu.VMEM((7, n_act, LANES), f32),
                pltpu.VMEM((16, n_act), f32),
                pltpu.VMEM((8, n_src), f32),
                dma((8,)),
                dma((n_line,)), dma((n_line,)),
                dma((n_line, n_grp)), dma((n_line, n_grp)),
                dma((n_grp,)), dma((n_grp,)),
                dma((n_core, n_grp)),
                dma((2,)),
            ],
            compiler_params=pltpu.CompilerParams(
                collective_id=0, has_side_effects=True, vmem_limit_bytes=60 * 1024 * 1024
            ),
        )(*args)
        batch = 2
        pos_vel, acc_jerk, pot = pl.pallas_call(
            functools.partial(finish, math.gcd(32, n_act), batch),
            out_shape=(
                jax.ShapeDtypeStruct((6, n_act), f32),
                jax.ShapeDtypeStruct((6, n_act), f32),
                jax.ShapeDtypeStruct((1, n_act), f32),
            ),
            in_specs=[hbm] * 3,
            out_specs=(hbm,) * 3,
            scratch_shapes=[
                pltpu.VMEM((n, n_chunk - 1, 8, LANES), f32),
                pltpu.VMEM((7, n_act, LANES), f32),
                pltpu.VMEM((16, n_act), f32),
                pltpu.VMEM((6, n_act, LANES), f32),
                pltpu.VMEM((n * (n_chunk - 1) + batch, 8, LANES), f32),
                pltpu.VMEM((7, n_act, LANES), f32),
                pltpu.VMEM((6, n_act), f32),
                pltpu.VMEM((6, n_act), f32),
                pltpu.VMEM((1, n_act), f32),
                dma((3,)),
                dma((3,)),
            ],
            compiler_params=pltpu.CompilerParams(vmem_limit_bytes=60 * 1024 * 1024),
        )(beyond.reshape(n, n_chunk - 1, 8, LANES), total, own)
        return pos_vel, acc_jerk, pot[0]

    split = P(None, ("grp", "dev"))
    flat = P(("grp", "dev"))
    return jax.shard_map(
        shards,
        mesh=mesh,
        in_specs=(split, split, split, split, flat, flat, flat, flat),
        out_specs=(split, split, flat),
        check_vma=False,
    )
```

profile of v0, /device:TPU:0, one launch (start us, length us, event | category | flops | bytes accessed | tf_op | source)
XLA Modules:
  0.0 21.0 jit_solution(229438735719493265)
XLA Ops:
  1.3 15.7 %shard_map.103 = (f32[2,4,4,1,8,128]{5,4,3,2,1,0:T(8,128)}, f32[7,128,128]{2,1,0:T(8,128)}, f32[16,128]{1,0:T(8,128)}) custom-call(f32[3,256]{1,0:T(4,128)} %pos_hbm.1, f32[3,256]{1,0:T(4,128)} %vel_hbm.1, f32[3,256]{1,0:T(4,128)} %acc_hbm.1, f32[3,256]{1,0:T(4,128)} %jerk_hbm.1, f32[1,256]{1,0:T(1,128)} %bitcast.6, s32[1,256]{1,0:T(1,128)} %bitcast.7, ...), custom_call_target="tpu_custom_call" | custom-call | tf_op jit(solution)/shard_map/pallas_call | solution.py:345
  16.9 4.0 %shard_map.104 = (f32[6,128]{1,0:T(8,128)}, f32[6,128]{1,0:T(8,128)}, f32[1,128]{1,0:T(1,128)}) custom-call(f32[32,1,8,128]{3,2,1,0:T(8,128)} %bitcast.5, f32[7,128,128]{2,1,0:T(8,128)} %get-tuple-element.10.total_hbm, f32[16,128]{1,0:T(8,128)} %get-tuple-element.11.own_hbm), custom_call_target="tpu_custom_call" | custom-call | tf_op jit(solution)/shard_map/pallas_call | solution.py:376
where the time goes:
time: 21 us
  Pallas kernels  19.7 us (94%)
  between operations  1.29 us (6%)
    pallas_call x1, Pallas kernels, shards(): pl.pallas_call(functools.partial(share, n_grp, n_line, n_core, math.gcd(1...  15.7 us
    pallas_call x1, Pallas kernels, shards(): pl.pallas_call(functools.partial(finish, math.gcd(32, n_act), batch), out...  4.05 us

commit v1 on v0

--- a/solution.py
+++ b/solution.py
@@ -172,6 +172,18 @@
 
         lax.fori_loop(0, n_line // batch, turn, 0)
 
+    def add_others(owner):
+        def turn(t, carry):
+            sweep(act, total, math.gcd(8, n_act), [
+                lambda c, origin=on_grp(k), at=t * batch + b: src[owner, origin, at, 0, c : c + 1, :]
+                for k in range(1, n_grp)
+                for b in range(batch)
+            ])
+            return carry
+
+        if n_grp > 1:
+            lax.fori_loop(0, n_line // batch, turn, 0)
+
     each(n_line, lambda k: line_copy(line, on_line(k)).start())
     to_groups(line)
 
@@ -215,16 +227,16 @@
         keep(core, origin).start()
 
     each(n_grp, forward)
-    each(n_grp, lambda k: add(core, on_grp(k)))
+    add_others(core)
 
     if n_core > 1:
         def last(k):
             origin = on_grp(k)
             core_copy(twin, origin).wait_recv()
             keep(twin, origin).start()
-            add(twin, origin)
 
         each(n_grp, last)
+        add_others(twin)
 
     total_copy = pltpu.make_async_copy(total, total_hbm, out_sem.at[1])
     total_copy.start()
@@ -372,9 +384,9 @@
                 collective_id=0, has_side_effects=True, vmem_limit_bytes=60 * 1024 * 1024
             ),
         )(*args)
-        batch = 2
+        batch = 4
         pos_vel, acc_jerk, pot = pl.pallas_call(
-            functools.partial(finish, math.gcd(32, n_act), batch),
+            functools.partial(finish, math.gcd(16, n_act), batch),
             out_shape=(
                 jax.ShapeDtypeStruct((6, n_act), f32),
                 jax.ShapeDtypeStruct((6, n_act), f32),

time: 21 us -> 21.5 us (1.024); the launches traced: 21 us -> 21.2 us
  no operation moved by 1% of the time
where the time goes in v1:
time: 21.5 us; the launch traced here: 21.2 us
  Pallas kernels  19.9 us (93%)
  between operations  1.29 us (6%)
    pallas_call x1, Pallas kernels, shards(): pl.pallas_call(functools.partial(share, n_grp, n_line, n_core, math.gcd(1...  15.8 us
    pallas_call x1, Pallas kernels, shards(): pl.pallas_call(functools.partial(finish, math.gcd(16, n_act), batch), out...  4.11 us

profile of v1, /device:TPU:0, one launch (start us, length us, event | category | flops | bytes accessed | tf_op | source)
XLA Modules:
  0.0 21.2 jit_solution(5431263224051390978)
XLA Ops:
  1.3 15.8 %shard_map.103 = (f32[2,4,4,1,8,128]{5,4,3,2,1,0:T(8,128)}, f32[7,128,128]{2,1,0:T(8,128)}, f32[16,128]{1,0:T(8,128)}) custom-call(f32[3,256]{1,0:T(4,128)} %pos_hbm.1, f32[3,256]{1,0:T(4,128)} %vel_hbm.1, f32[3,256]{1,0:T(4,128)} %acc_hbm.1, f32[3,256]{1,0:T(4,128)} %jerk_hbm.1, f32[1,256]{1,0:T(1,128)} %bitcast.6, s32[1,256]{1,0:T(1,128)} %bitcast.7, ...), custom_call_target="tpu_custom_call" | custom-call | tf_op jit(solution)/shard_map/pallas_call | solution.py:357
  17.1 4.1 %shard_map.104 = (f32[6,128]{1,0:T(8,128)}, f32[6,128]{1,0:T(8,128)}, f32[1,128]{1,0:T(1,128)}) custom-call(f32[32,1,8,128]{3,2,1,0:T(8,128)} %bitcast.5, f32[7,128,128]{2,1,0:T(8,128)} %get-tuple-element.10.total_hbm, f32[16,128]{1,0:T(8,128)} %get-tuple-element.11.own_hbm), custom_call_target="tpu_custom_call" | custom-call | tf_op jit(solution)/shard_map/pallas_call | solution.py:388

commit v2 on v0

--- a/solution.py
+++ b/solution.py
@@ -192,6 +192,15 @@
     own_copy.start()
     spread(own, act)
 
+    def add_near(ks):
+        sweep(act, total, rows, [
+            lambda c, at=on_line(k), chunk=chunk: src[core, grp, at, chunk, c : c + 1, :]
+            for k in ks for chunk in range(n_chunk)
+        ])
+
+    near = min(n_line, batch)
+    add_near([0])
+
     def pass_on(k):
         line_copy(on_line(k), on_line(k)).wait_recv()
         to_groups(on_line(k))
@@ -200,7 +209,13 @@
     if n_core > 1:
         core_copy(core, grp).start()
     keep(core, grp).start()
-    add(core, grp)
+    add_near(range(1, near))
+    if n_line > near:
+        def further(k, carry):
+            add_near([k])
+            return carry
+
+        lax.fori_loop(near, n_line, further, 0)
     if n_core > 1:
         core_copy(twin, grp).wait_recv()
         keep(twin, grp).start()
@@ -249,7 +264,7 @@
 
 
 def finish(
-    rows, batch,
+    n_grp, n_line, n_core, rows, batch,
     beyond_hbm, total_hbm, own_hbm,
     pos_vel_hbm, acc_jerk_hbm, pot_hbm,
     beyond, total, own, act, packed, more, pos_vel_ref, acc_jerk_ref, pot_ref, load_sem, store_sem,
@@ -270,10 +285,14 @@
 
     unroll = math.gcd(8, n)
 
+    near = (lax.rem(lax.axis_index("dev"), n_core) * n_grp + lax.axis_index("grp")) * n_line
+
     def pack(turn, carry):
         filled, now = carry
         counts = [beyond[turn * unroll + b, 0, 7, 0].astype(jnp.int32) for b in range(unroll)]
         for b in range(unroll):
+            at = turn * unroll + b
+            counts[b] = jnp.where((at >= near) & (at < near + n_line), 0, counts[b])
             for chunk in range(n_beyond):
                 many = jnp.minimum(jnp.maximum(counts[b] - (chunk + 1) * LANES, 0), LANES)
                 start = lax.rem(filled, LANES)
@@ -374,7 +393,7 @@
         )(*args)
         batch = 2
         pos_vel, acc_jerk, pot = pl.pallas_call(
-            functools.partial(finish, math.gcd(32, n_act), batch),
+            functools.partial(finish, n_grp, n_line, n_core, math.gcd(32, n_act), batch),
             out_shape=(
                 jax.ShapeDtypeStruct((6, n_act), f32),
                 jax.ShapeDtypeStruct((6, n_act), f32),

time: 21 us -> 20.5 us (0.976)
  Pallas kernels: 19.7 us -> 19.1 us
    pallas_call x1, Pallas kernels: 4.05 us -> 3.43 us  [shards(): pl.pallas_call(functools.partial(finish, n_grp, n_line, n_core, math.gcd(...]
where the time goes in v2:
time: 20.5 us; the launch traced here: 20.4 us
  Pallas kernels  19.1 us (93%)
  between operations  1.29 us (6%)
    pallas_call x1, Pallas kernels, shards(): pl.pallas_call(functools.partial(share, n_grp, n_line, n_core, math.gcd(1...  15.7 us
    pallas_call x1, Pallas kernels, shards(): pl.pallas_call(functools.partial(finish, n_grp, n_line, n_core, math.gcd(...  3.43 us

profile of v2, /device:TPU:0, one launch (start us, length us, event | category | flops | bytes accessed | tf_op | source)
XLA Modules:
  0.0 20.4 jit_solution(1701427759362646052)
XLA Ops:
  1.3 15.7 %shard_map.103 = (f32[2,4,4,1,8,128]{5,4,3,2,1,0:T(8,128)}, f32[7,128,128]{2,1,0:T(8,128)}, f32[16,128]{1,0:T(8,128)}) custom-call(f32[3,256]{1,0:T(4,128)} %pos_hbm.1, f32[3,256]{1,0:T(4,128)} %vel_hbm.1, f32[3,256]{1,0:T(4,128)} %acc_hbm.1, f32[3,256]{1,0:T(4,128)} %jerk_hbm.1, f32[1,256]{1,0:T(1,128)} %bitcast.6, s32[1,256]{1,0:T(1,128)} %bitcast.7, ...), custom_call_target="tpu_custom_call" | custom-call | tf_op jit(solution)/shard_map/pallas_call | solution.py:364
  17.0 3.4 %shard_map.104 = (f32[6,128]{1,0:T(8,128)}, f32[6,128]{1,0:T(8,128)}, f32[1,128]{1,0:T(1,128)}) custom-call(f32[32,1,8,128]{3,2,1,0:T(8,128)} %bitcast.5, f32[7,128,128]{2,1,0:T(8,128)} %get-tuple-element.10.total_hbm, f32[16,128]{1,0:T(8,128)} %get-tuple-element.11.own_hbm), custom_call_target="tpu_custom_call" | custom-call | tf_op jit(solution)/shard_map/pallas_call | solution.py:395

commit v3 on v2

--- a/solution.py
+++ b/solution.py
@@ -391,9 +391,9 @@
                 collective_id=0, has_side_effects=True, vmem_limit_bytes=60 * 1024 * 1024
             ),
         )(*args)
-        batch = 2
+        batch = 4
         pos_vel, acc_jerk, pot = pl.pallas_call(
-            functools.partial(finish, n_grp, n_line, n_core, math.gcd(32, n_act), batch),
+            functools.partial(finish, n_grp, n_line, n_core, math.gcd(16, n_act), batch),
             out_shape=(
                 jax.ShapeDtypeStruct((6, n_act), f32),
                 jax.ShapeDtypeStruct((6, n_act), f32),

time: 20.5 us -> 20.9 us (1.020)
  Pallas kernels: 19.1 us -> 19.4 us
    pallas_call x1, Pallas kernels: 3.43 us -> 3.69 us  [shards(): pl.pallas_call(functools.partial(finish, n_grp, n_line, n_core, math.gcd(...]
where the time goes in v3:
time: 20.9 us; the launch traced here: 20.6 us
  Pallas kernels  19.4 us (93%)
  between operations  1.29 us (6%)
    pallas_call x1, Pallas kernels, shards(): pl.pallas_call(functools.partial(share, n_grp, n_line, n_core, math.gcd(1...  15.7 us
    pallas_call x1, Pallas kernels, shards(): pl.pallas_call(functools.partial(finish, n_grp, n_line, n_core, math.gcd(...  3.69 us

profile of v3, /device:TPU:0, one launch (start us, length us, event | category | flops | bytes accessed | tf_op | source)
XLA Modules:
  0.0 20.6 jit_solution(6502347698278238979)
XLA Ops:
  1.3 15.7 %shard_map.103 = (f32[2,4,4,1,8,128]{5,4,3,2,1,0:T(8,128)}, f32[7,128,128]{2,1,0:T(8,128)}, f32[16,128]{1,0:T(8,128)}) custom-call(f32[3,256]{1,0:T(4,128)} %pos_hbm.1, f32[3,256]{1,0:T(4,128)} %vel_hbm.1, f32[3,256]{1,0:T(4,128)} %acc_hbm.1, f32[3,256]{1,0:T(4,128)} %jerk_hbm.1, f32[1,256]{1,0:T(1,128)} %bitcast.6, s32[1,256]{1,0:T(1,128)} %bitcast.7, ...), custom_call_target="tpu_custom_call" | custom-call | tf_op jit(solution)/shard_map/pallas_call | solution.py:364
  17.0 3.7 %shard_map.104 = (f32[6,128]{1,0:T(8,128)}, f32[6,128]{1,0:T(8,128)}, f32[1,128]{1,0:T(1,128)}) custom-call(f32[32,1,8,128]{3,2,1,0:T(8,128)} %bitcast.5, f32[7,128,128]{2,1,0:T(8,128)} %get-tuple-element.10.total_hbm, f32[16,128]{1,0:T(8,128)} %get-tuple-element.11.own_hbm), custom_call_target="tpu_custom_call" | custom-call | tf_op jit(solution)/shard_map/pallas_call | solution.py:395
